TPU v7x, 32 devices: a whole 2x2x4 slice. The times are simulated.
32 devices in a mesh: expert: 8 (over z, x), hidden: 4 (over y, core).
Axes of the slice: x: 2, y: 2, z: 4, core: 2. Of those that a mesh axis runs over, the one named last changes fastest.
Arguments:
- tokens: bfloat16 [128, 7168], P('expert', 'hidden'), may hold values from -6 to 6
- routes: int32 [128, 8], P('expert'), may hold values from 0 to 15, as said below
- combine: float32 [128, 8], P('expert'), may hold values from 0.05 to 0.5
- w_gate: bfloat16 [16, 7168, 1024], P('expert', None, 'hidden'), may hold values from -0.0625 to 0.0625
- w_up: bfloat16 [16, 7168, 1024], P('expert', None, 'hidden'), may hold values from -0.0625 to 0.0625
- w_down: bfloat16 [16, 1024, 7168], P('expert', 'hidden'), may hold values from -0.1875 to 0.1875
- cotangent: bfloat16 [128, 7168], P('expert', 'hidden'), may hold values from -6 to 6
Outputs:
- output: bfloat16 [128, 7168], P('expert', 'hidden')
- grad_tokens: bfloat16 [128, 7168], P('expert', 'hidden')
Inputs may be any that keep to these rules, and one draw needn't show every extreme that they name: `routes`: each row names 8 different experts. In each aligned block of 16 rows (the rows of one device) no expert is named by more than 16 rows, and the same expert is named by exactly 16 rows in every block.
All inputs are finite; a program needn't handle non-finite values.
Results may differ from a plain program's by a relative error of at most 0.012.
Values may be sent and summed in bfloat16 or wider, within the bound.
A program may use at most 128 MiB of HBM per device.

v0:
```python
import jax
import jax.numpy as jnp
from jax import lax
from jax.sharding import PartitionSpec as P


def per_device(tokens, routes, combine, w_gate, w_up, w_down, cotangent):
    tok_rows = tokens.shape[0]
    top_count = routes.shape[1]
    local_experts = w_gate.shape[0]
    sources = lax.axis_size("expert")
    experts = local_experts * sources
    pair_count = tok_rows * top_count
    capacity = 2 * pair_count // experts
    flat_routes = routes.reshape(pair_count)
    onehot = (flat_routes[:, None] == jnp.arange(experts, dtype=jnp.int32)[None, :]).astype(
        jnp.int32
    )
    slot_rank = jnp.sum((jnp.cumsum(onehot, axis=0) - 1) * onehot, axis=1)
    target = flat_routes * capacity + slot_rank
    slot_table = (
        jnp.full((experts * capacity,), pair_count, jnp.int32)
        .at[target]
        .set(jnp.arange(pair_count, dtype=jnp.int32))
    )
    source_rows = slot_table // top_count

    def pack_rows(values):
        padded = jnp.concatenate([values, jnp.zeros((1, values.shape[1]), values.dtype)], axis=0)
        return padded[source_rows].reshape(experts, capacity, values.shape[1])

    def to_local(arrived):
        columns = arrived.shape[2]
        sectioned = arrived.reshape(sources, local_experts, capacity, columns).transpose(1, 0, 2, 3)
        return sectioned.reshape(local_experts, sources * capacity, columns)

    def to_global(leaving):
        columns = leaving.shape[2]
        sectioned = leaving.reshape(local_experts, sources, capacity, columns).transpose(1, 0, 2, 3)
        return sectioned.reshape(experts, capacity, columns)

    def unpack(returned):
        flattened = returned.reshape(experts * capacity, returned.shape[2])
        picked = (
            flattened[target].astype(jnp.float32).reshape(tok_rows, top_count, returned.shape[2])
        )
        return jnp.sum(picked * combine[:, :, None], axis=1).astype(jnp.bfloat16)

    full_tokens, full_grads = (
        lax.all_gather(tokens, "hidden", axis=1, tiled=True),
        lax.all_gather(cotangent, "hidden", axis=1, tiled=True),
    )
    arrived_x, arrived_dy = (
        lax.all_to_all(pack_rows(full_tokens), "expert", split_axis=0, concat_axis=0, tiled=True),
        lax.all_to_all(pack_rows(full_grads), "expert", split_axis=0, concat_axis=0, tiled=True),
    )
    arrived_x = to_local(arrived_x)
    arrived_dy = to_local(arrived_dy)
    gate_pre = jnp.einsum("erd,edf->erf", arrived_x, w_gate, preferred_element_type=jnp.float32)
    up_pre = jnp.einsum("erd,edf->erf", arrived_x, w_up, preferred_element_type=jnp.float32)
    back_hidden = jnp.einsum("erd,efd->erf", arrived_dy, w_down, preferred_element_type=jnp.float32)
    sigmoid_gate = jax.nn.sigmoid(gate_pre)
    activated = gate_pre * sigmoid_gate
    hidden_act = (activated * up_pre).astype(jnp.bfloat16)
    out_terms = jnp.einsum(
        "erf,efd->erd", hidden_act, w_down, preferred_element_type=jnp.float32
    ).astype(jnp.bfloat16)
    grad_gate = (
        back_hidden * up_pre * sigmoid_gate * (1.0 + gate_pre * (1.0 - sigmoid_gate))
    ).astype(jnp.bfloat16)
    grad_up = (back_hidden * activated).astype(jnp.bfloat16)
    out_share = (
        lax.psum_scatter(out_terms, "hidden", scatter_dimension=2, tiled=True)
        .astype(jnp.float32)
        .astype(jnp.bfloat16)
    )
    out_back = lax.all_to_all(
        to_global(out_share), "expert", split_axis=0, concat_axis=0, tiled=True
    )
    grad_terms = jnp.einsum("erf,edf->erd", grad_gate, w_gate, preferred_element_type=jnp.float32)
    grad_terms = grad_terms + jnp.einsum(
        "erf,edf->erd", grad_up, w_up, preferred_element_type=jnp.float32
    )
    grad_share = lax.psum_scatter(
        grad_terms.astype(jnp.bfloat16), "hidden", scatter_dimension=2, tiled=True
    )
    grad_back = lax.all_to_all(
        to_global(grad_share), "expert", split_axis=0, concat_axis=0, tiled=True
    )
    return (unpack(out_back), unpack(grad_back))


def solution(mesh):
    return jax.shard_map(
        per_device,
        mesh=mesh,
        in_specs=(
            P("expert", "hidden"),
            P("expert", None),
            P("expert", None),
            P("expert", None, "hidden"),
            P("expert", None, "hidden"),
            P("expert", "hidden", None),
            P("expert", "hidden"),
        ),
        out_specs=(P("expert", "hidden"), P("expert", "hidden")),
        check_vma=False,
    )
```

profile of v0, /device:TPU:0, one launch (start us, length us, event | category | flops | bytes accessed | tf_op | source)
XLA Modules:
  0.0 345.9 jit_solution(1622164715851073703)
XLA Ops:
  10.3 7.3 %all_gather.6 = bf16[16,7168]{1,0:T(8,128)(2,1)S(1)} all-gather(bf16[16,1792]{1,0:T(8,128)(2,1)} %param.7), channel_id=1, replica_groups=mesh['expert'=8,'hidden'=4] {'hidden'}, dimensions={1}, use_global_device_ids=true | all-gather | bytes 286720 | tf_op jit(solution)/shard_map/all_gather | solution.py:50
  17.6 4.8 %gather_fusion = bf16[256,7168]{1,0:T(8,128)(2,1)} fusion(bf16[17,7168]{1,0:T(8,128)(2,1)S(1)} %concatenate.6, s32[1024]{0:T(1024)S(1)} %pad_clamp_fusion.1), kind=kCustom, calls=%fused_computation | custom fusion | bytes 7341056 | tf_op jit(solution)/shard_map/gather | solution.py:30
  22.4 6.0 %all-to-all-start = ((bf16[16,16,7168]{2,1,0:T(8,128)(2,1)}), bf16[16,16,7168]{2,1,0:T(8,128)(2,1)}, u32[]{:S(2)}, u32[]{:S(2)}) async-start(bf16[16,16,7168]{2,1,0:T(8,128)(2,1)} %bitcast.50), calls=%async_computation | async-start | bytes 7340032 | tf_op jit(solution)/shard_map/all_to_all | solution.py:54
  28.5 5.7 %all_gather.7 = bf16[16,7168]{1,0:T(8,128)(2,1)S(1)} all-gather(bf16[16,1792]{1,0:T(8,128)(2,1)S(1)} %copy-done), channel_id=1, replica_groups=mesh['expert'=8,'hidden'=4] {'hidden'}, dimensions={1}, use_global_device_ids=true | all-gather | bytes 286720 | tf_op jit(solution)/shard_map/all_gather | solution.py:51
  34.2 4.7 %gather_fusion.2 = bf16[256,7168]{1,0:T(8,128)(2,1)} fusion(bf16[17,7168]{1,0:T(8,128)(2,1)S(1)} %concatenate.7, s32[1024]{0:T(1024)S(1)} %pad_clamp_fusion.1), kind=kCustom, calls=%fused_computation.2 | custom fusion | bytes 7341056 | tf_op jit(solution)/shard_map/gather | solution.py:30
  38.9 72.1 %all-to-all-done = bf16[16,16,7168]{2,1,0:T(8,128)(2,1)} async-done(((bf16[16,16,7168]{2,1,0:T(8,128)(2,1)}), bf16[16,16,7168]{2,1,0:T(8,128)(2,1)}, u32[]{:S(2)}, u32[]{:S(2)}) %all-to-all-start) | async-done | bytes 3670048 | tf_op jit(solution)/shard_map/all_to_all | solution.py:54
  111.0 4.5 %all-to-all-start.2 = ((bf16[16,16,7168]{2,1,0:T(8,128)(2,1)}), bf16[16,16,7168]{2,1,0:T(8,128)(2,1)}, u32[]{:S(2)}, u32[]{:S(2)}) async-start(bf16[16,16,7168]{2,1,0:T(8,128)(2,1)} %bitcast.49), calls=%async_computation.3 | async-start | bytes 7340032 | tf_op jit(solution)/shard_map/all_to_all | solution.py:55
  115.7 2.5 copy.14
  118.3 4.4 %fusion.15 = f32[2,128,256]{2,1,0:T(8,128)S(1)} fusion(bf16[2,128,7168]{2,1,0:T(8,128)(2,1)S(1)} %bitcast.41, bf16[2,7168,256]{2,1,0:T(8,128)(2,1)} %param.10), kind=kOutput, calls=%fused_computation.38 | convolution fusion | flops 939524096 | bytes 11272192 | tf_op jit(solution)/shard_map/erd,edf->erf/dot_general | solution.py:59
  122.7 1.1 fusion.16
  123.9 73.2 %all-to-all-done.2 = bf16[16,16,7168]{2,1,0:T(8,128)(2,1)} async-done(((bf16[16,16,7168]{2,1,0:T(8,128)(2,1)}), bf16[16,16,7168]{2,1,0:T(8,128)(2,1)}, u32[]{:S(2)}, u32[]{:S(2)}) %all-to-all-start.2) | async-done | bytes 3670048 | tf_op jit(solution)/shard_map/all_to_all | solution.py:55
  197.1 2.3 copy.17
  199.5 5.8 %fusion.17 = f32[2,128,256]{2,1,0:T(8,128)S(1)} fusion(bf16[2,128,7168]{2,1,0:T(8,128)(2,1)S(1)} %bitcast.51, bf16[2,256,7168]{2,1,0:T(8,128)(2,1)} %param.12), kind=kOutput, calls=%fused_computation.40 | convolution fusion | flops 939524096 | bytes 11272192 | tf_op jit(solution)/shard_map/erd,efd->erf/dot_general | solution.py:61
  205.3 8.7 %fusion.4 = f32[2,128,7168]{2,1,0:T(8,128)} fusion(bf16[2,7168,256]{2,1,0:T(8,128)(2,1)} %param.10, f32[2,128,256]{2,1,0:T(8,128)S(1)} %fusion.15, f32[2,128,256]{2,1,0:T(8,128)S(1)} %fusion.17, f32[2,128,256]{2,1,0:T(8,128)S(1)} %fusion.16), kind=kOutput, calls=%fused_computation.17 | convolution fusion | flops 940179456 | bytes 15466496 | tf_op jit(solution)/shard_map/erf,edf->erd/dot_general | solution.py:80
  214.0 7.5 %fusion = bf16[2,128,7168]{2,1,0:T(8,128)(2,1)} fusion(f32[2,128,7168]{2,1,0:T(8,128)} %fusion.4, bf16[2,7168,256]{2,1,0:T(8,128)(2,1)S(1)} %bitcast.46, f32[2,128,256]{2,1,0:T(8,128)S(1)} %fusion.17, f32[2,128,256]{2,1,0:T(8,128)S(1)} %fusion.15), kind=kOutput, calls=%fused_computation.7 | convolution fusion | flops 943587328 | bytes 18874368 | tf_op jit(solution)/shard_map/erf,edf->erd/dot_general | solution.py:81
  221.6 6.1 %convolution_convert_fusion = bf16[2,128,7168]{2,1,0:T(8,128)(2,1)} fusion(bf16[2,256,7168]{2,1,0:T(8,128)(2,1)} %param.12, f32[2,128,256]{2,1,0:T(8,128)S(1)} %fusion.16, f32[2,128,256]{2,1,0:T(8,128)S(1)} %fusion.15), kind=kOutput, calls=%fused_computation.6 | convolution fusion | flops 941752320 | bytes 11534336 | tf_op jit(solution)/shard_map/erf,efd->erd/dot_general | solution.py:65
  227.6 34.3 %reduce-scatter.5.cloned.1.call-done = bf16[2,128,1792]{2,1,0:T(8,128)(2,1)} async-done(((bf16[2,128,7168]{2,1,0:T(8,128)(2,1)}), bf16[2,128,1792]{2,1,0:T(8,128)(2,1)}) %reduce-scatter.5.cloned.1.call-update) | async-done | bytes 917520 | tf_op jit(solution)/shard_map/reduce_scatter | solution.py:84
  262.0 2.2 copy.18
  264.2 5.5 %all-to-all-start.3 = ((bf16[16,16,1792]{2,1,0:T(8,128)(2,1)}), bf16[16,16,1792]{2,1,0:T(8,128)(2,1)S(1)}, u32[]{:S(2)}, u32[]{:S(2)}) async-start(bf16[16,16,1792]{2,1,0:T(8,128)(2,1)} %bitcast.17), calls=%async_computation.5 | async-start | bytes 1835008 | tf_op jit(solution)/shard_map/all_to_all | solution.py:87
  269.7 36.3 %reduce-scatter.3.cloned.1.call-done = bf16[2,128,1792]{2,1,0:T(8,128)(2,1)} async-done(((bf16[2,128,7168]{2,1,0:T(8,128)(2,1)}), bf16[2,128,1792]{2,1,0:T(8,128)(2,1)}) %reduce-scatter.3.cloned.1.call-update) | async-done | bytes 917520 | tf_op jit(solution)/shard_map/reduce_scatter | solution.py:73
  305.9 2.2 copy.15
  308.1 5.5 %all-to-all-start.1 = ((bf16[16,16,1792]{2,1,0:T(8,128)(2,1)}), bf16[16,16,1792]{2,1,0:T(8,128)(2,1)S(1)}, u32[]{:S(2)}, u32[]{:S(2)}) async-start(bf16[16,16,1792]{2,1,0:T(8,128)(2,1)} %bitcast.8), calls=%async_computation.2 | async-start | bytes 1835008 | tf_op jit(solution)/shard_map/all_to_all | solution.py:77
  314.7 22.0 %all-to-all-done.1 = bf16[16,16,1792]{2,1,0:T(8,128)(2,1)S(1)} async-done(((bf16[16,16,1792]{2,1,0:T(8,128)(2,1)}), bf16[16,16,1792]{2,1,0:T(8,128)(2,1)S(1)}, u32[]{:S(2)}, u32[]{:S(2)}) %all-to-all-start.1) | async-done | bytes 917536 | tf_op jit(solution)/shard_map/all_to_all | solution.py:77
  337.6 1.4 fusion.1
  (38 shorter events, 5.5 us)
Async XLA Ops:
  22.4 6.0 %copy-start = (bf16[16,1792]{1,0:T(8,128)(2,1)S(1)}, bf16[16,1792]{1,0:T(8,128)(2,1)}, u32[]{:S(2)}) copy-start(bf16[16,1792]{1,0:T(8,128)(2,1)} %param.13) | copy-start | bytes 172036
  22.4 88.6 %all-to-all-start = ((bf16[16,16,7168]{2,1,0:T(8,128)(2,1)}), bf16[16,16,7168]{2,1,0:T(8,128)(2,1)}, u32[]{:S(2)}, u32[]{:S(2)}) async-start(bf16[16,16,7168]{2,1,0:T(8,128)(2,1)} %bitcast.50), calls=%async_computation | async-start | bytes 7340032 | tf_op jit(solution)/shard_map/all_to_all | solution.py:54
  111.0 86.1 %all-to-all-start.2 = ((bf16[16,16,7168]{2,1,0:T(8,128)(2,1)}), bf16[16,16,7168]{2,1,0:T(8,128)(2,1)}, u32[]{:S(2)}, u32[]{:S(2)}) async-start(bf16[16,16,7168]{2,1,0:T(8,128)(2,1)} %bitcast.49), calls=%async_computation.3 | async-start | bytes 7340032 | tf_op jit(solution)/shard_map/all_to_all | solution.py:55
  115.5 146.5 %reduce-scatter.5.cloned.1.call-start = ((), (), s32[]{:S(2)}) async-start(), calls=%async_computation.7 | async-start | bytes 4587520 | tf_op jit(solution)/shard_map/reduce_scatter | solution.py:84
  115.7 7.0 %slice-start = ((s8[7340032]{0:T(1024)(128)(4,1)}), s8[4194304]{0:T(1024)(128)(4,1)S(1)}, s32[]{:S(2)}) async-start(s8[7340032]{0:T(1024)(128)(4,1)} %bitcast.43), calls=%async_computation.8 | async-start | bytes 8388608
  118.3 4.5 %slice-start.1 = ((s8[7340032]{0:T(1024)(128)(4,1)}), s8[3145728]{0:T(1024)(128)(4,1)S(1)}, s32[]{:S(2)}) async-start(s8[7340032]{0:T(1024)(128)(4,1)} %bitcast.43), calls=%async_computation.9 | async-start | bytes 6291456
  199.4 14.5 %slice-start.2 = ((s8[7340032]{0:T(1024)(128)(4,1)}), s8[4194304]{0:T(1024)(128)(4,1)S(1)}, s32[]{:S(2)}) async-start(s8[7340032]{0:T(1024)(128)(4,1)} %bitcast.45), calls=%async_computation.10 | async-start | bytes 8388608
  205.3 8.7 %slice-start.3 = ((s8[7340032]{0:T(1024)(128)(4,1)}), s8[3145728]{0:T(1024)(128)(4,1)S(1)}, s32[]{:S(2)}) async-start(s8[7340032]{0:T(1024)(128)(4,1)} %bitcast.45), calls=%async_computation.11 | async-start | bytes 6291456
  221.5 84.4 %reduce-scatter.3.cloned.1.call-start = ((), (), s32[]{:S(2)}) async-start(), calls=%async_computation.6 | async-start | bytes 4587520 | tf_op jit(solution)/shard_map/reduce_scatter | solution.py:73
  227.6 86.0 %copy-start.1 = (f32[16,8]{0,1:T(8,128)S(1)}, f32[16,8]{0,1:T(8,128)}, u32[]{:S(2)}) copy-start(f32[16,8]{0,1:T(8,128)} %param.9) | copy-start | bytes 1540
  264.2 44.0 %all-to-all-start.3 = ((bf16[16,16,1792]{2,1,0:T(8,128)(2,1)}), bf16[16,16,1792]{2,1,0:T(8,128)(2,1)S(1)}, u32[]{:S(2)}, u32[]{:S(2)}) async-start(bf16[16,16,1792]{2,1,0:T(8,128)(2,1)} %bitcast.17), calls=%async_computation.5 | async-start | bytes 1835008 | tf_op jit(solution)/shard_map/all_to_all | solution.py:87
  308.1 28.5 %all-to-all-start.1 = ((bf16[16,16,1792]{2,1,0:T(8,128)(2,1)}), bf16[16,16,1792]{2,1,0:T(8,128)(2,1)S(1)}, u32[]{:S(2)}, u32[]{:S(2)}) async-start(bf16[16,16,1792]{2,1,0:T(8,128)(2,1)} %bitcast.8), calls=%async_computation.2 | async-start | bytes 1835008 | tf_op jit(solution)/shard_map/all_to_all | solution.py:77
Sparse Core Ops, SparseCore 0:
  221.6 40.3 reduce-scatter.4
  264.7 41.2 reduce-scatter.2
where the time goes:
time: 347 us; the launch traced here: 346 us
  waiting for transfers between devices  238 us (69%)
  matrix products  33.6 us (10%)
  local copies, waits for them, and re-layouts  22.7 us (7%)
  starting transfers between devices  21.8 us (6%)
  between operations  14.2 us (4%)
  blocking collectives  13 us (4%)
    all_to_all x1, waiting for transfers between devices, per_device(): lax.all_to_all(pack_rows(full_grads), 'expert', split_axis=0, concat_axis...  73.2 us
    all_to_all x1, waiting for transfers between devices, per_device(): lax.all_to_all(pack_rows(full_tokens), 'expert', split_axis=0, concat_axi...  72.1 us
    reduce_scatter x1, waiting for transfers between devices, per_device(): lax.psum_scatter(out_terms, 'hidden', scatter_dimension=2, tiled=True)  36.3 us
    reduce_scatter x1, waiting for transfers between devices, per_device(): lax.psum_scatter(grad_terms.astype(jnp.bfloat16), 'hidden', scatter_dimen...  34.3 us
    all_to_all x1, waiting for transfers between devices, per_device(): lax.all_to_all(to_global(out_share), 'expert', split_axis=0, concat_axis=...  22 us
    gather x2, local copies, waits for them, and re-layouts, pack_rows(): return padded[source_rows].reshape(experts, capacity, values.shape[1])  9.48 us
    dot_general x1, matrix products, per_device(): jnp.einsum('erf,edf->erd', grad_gate, w_gate, preferred_element_type=jnp....  8.67 us
    dot_general x1, matrix products, per_device(): jnp.einsum('erf,edf->erd', grad_up, w_up, preferred_element_type=jnp.floa...  7.53 us
  transfers between devices with their start and end apart: 6, of which 5 were waited for; matrix products, arithmetic and copies ran while one was open for 7% of the time, Pallas kernels for 0%

commit v1 on v0

--- a/solution.py
+++ b/solution.py
@@ -1,6 +1,8 @@
 import jax
 import jax.numpy as jnp
 from jax import lax
+from jax.experimental import pallas as pl
+from jax.experimental.pallas import tpu as pltpu
 from jax.sharding import PartitionSpec as P
 
 
@@ -90,19 +92,345 @@
     return (unpack(out_back), unpack(grad_back))
 
 
+SPECS = (
+    P("expert", "hidden"),
+    P("expert", None),
+    P("expert", None),
+    P("expert", None, "hidden"),
+    P("expert", None, "hidden"),
+    P("expert", "hidden", None),
+    P("expert", "hidden"),
+)
+MESH = pl.DeviceIdType.MESH
+ROWS = 16
+ORDER = (1, 3, 2)
+F32 = jnp.float32
+BF16 = jnp.bfloat16
+GT, GC, GW, RO, RG = 0, 31, 62, 66, 83
+COPIES = 100
+
+
+def dot_nt(a, b):
+    return lax.dot_general(a, b, (((1,), (1,)), ((), ())), preferred_element_type=F32)
+
+
+def kernel(
+    tok, cot, routes, comb, wg_hbm, wu_hbm, wd_hbm, out, grad,
+    X, Y, wg, wu, wd, cb, gacc, uacc, bacc, H, G,
+    PO, PG, RcO, RcG, RyO, RxO, RzO, RxG, RyG, RzG, ssem, rsem, lsem,
+):
+    e, h = lax.axis_index("expert"), lax.axis_index("hidden")
+    z, x, y, c = e // 2, e % 2, h // 2, h % 2
+    xn, yn, cn = 1 - x, 1 - y, 1 - c
+    cols = tok.shape[1]
+    units = wd_hbm.shape[1]
+    dev_x, dev_y, dev_s = (z * 2 + xn, h), (e, yn * 2 + c), (e, y * 2 + cn)
+    dev_z = {i: (((z + i) % 4) * 2 + x, h) for i in ORDER}
+
+    def rows(xx, zz):
+        return pl.ds(pl.multiple_of((xx * 4 + zz) * ROWS, ROWS), ROWS)
+
+    def half(zz):
+        return pl.ds(pl.multiple_of(zz * ROWS, ROWS), ROWS)
+
+    started = []
+
+    def send(src, dst, k, dev):
+        copy = pltpu.make_async_remote_copy(
+            src_ref=src, dst_ref=dst, send_sem=ssem.at[k], recv_sem=rsem.at[k],
+            device_id=dev, device_id_type=MESH,
+        )
+        copy.start()
+        started.append(copy)
+
+    def arrive(ref, k, dev):
+        pltpu.make_async_remote_copy(
+            src_ref=ref, dst_ref=ref, send_sem=ssem.at[k], recv_sem=rsem.at[k],
+            device_id=dev, device_id_type=MESH,
+        ).wait_recv()
+
+    barrier = pltpu.get_barrier_semaphore()
+    partners = [dev_x, dev_y, dev_s] + [dev_z[i] for i in ORDER]
+    for dev in partners:
+        pl.semaphore_signal(barrier, inc=1, device_id=dev, device_id_type=MESH)
+
+    X[h, rows(x, z), :] = tok[...]
+    Y[h, rows(x, z), :] = cot[...]
+    lane = lax.broadcasted_iota(jnp.int32, (ROWS, 128), 1)
+    expert = jnp.where(lane < 16, lane, lane - 16)
+    dense = jnp.zeros((ROWS, 128), F32)
+    for k in range(routes.shape[1]):
+        dense = dense + jnp.where(expert == routes[:, k : k + 1], comb[:, k : k + 1], 0.0)
+    high = dense.astype(BF16)
+    low = (dense - high.astype(F32)).astype(BF16)
+    cb[rows(x, z), :] = jnp.where(lane < 16, high.astype(F32), low.astype(F32)).astype(BF16)
+    pl.semaphore_wait(barrier, len(partners))
+
+    def near(i):
+        return (z - i) % 4
+
+    def blk(buf, yy, cc, xx, zz):
+        return buf.at[yy * 2 + cc, rows(xx, zz), :]
+
+    def first(arr, i):
+        buf, base, dev1, dev2 = arr
+        ref = blk(buf, y, c, x, near(i))
+        send(ref, ref, base + 3 + i, dev1)
+        send(ref, ref, base + 7 + i, dev2)
+
+    def sib(arr, yo, xo, i):
+        ref = blk(arr[0], (y, yn)[yo], c, (x, xn)[xo], near(i))
+        send(ref, ref, arr[1] + 15 + 8 * yo + 4 * xo + i, dev_s)
+
+    def sib_arrive(arr, yo, xo, i):
+        ref = blk(arr[0], (y, yn)[yo], cn, (x, xn)[xo], near(i))
+        arrive(ref, arr[1] + 15 + 8 * yo + 4 * xo + i, dev_s)
+
+    TOKS, COTS = (X, GT, dev_x, dev_y), (Y, GC, dev_y, dev_x)
+    BOTH = (TOKS, COTS)
+    for i in ORDER:
+        for arr in BOTH:
+            ref = blk(arr[0], y, c, x, z)
+            send(ref, ref, arr[1] + i - 1, dev_z[i])
+        if i == ORDER[0]:
+            for arr in BOTH:
+                first(arr, 0)
+    for i in ORDER:
+        ref = cb.at[rows(x, z), :]
+        send(ref, ref, GW + i - 1, dev_z[i])
+    for arr in BOTH:
+        sib(arr, 0, 0, 0)
+
+    wcopies = [
+        pltpu.make_async_copy(wg_hbm, wg, lsem.at[0]),
+        pltpu.make_async_copy(wu_hbm, wu, lsem.at[1]),
+    ]
+    for hh in range(4):
+        for j in range(2):
+            wcopies.append(
+                pltpu.make_async_copy(
+                    wd_hbm.at[j, :, pl.ds(hh * cols, cols)],
+                    wd.at[hh, pl.ds(j * units, units), :],
+                    lsem.at[2 + hh * 2 + j],
+                )
+            )
+    for copy in wcopies:
+        copy.start()
+
+    for i in ORDER:
+        for arr in BOTH:
+            arrive(blk(arr[0], y, c, x, near(i)), arr[1] + i - 1, dev_z[i])
+            first(arr, i)
+            sib(arr, 0, 0, i)
+    for i in ORDER:
+        arrive(cb.at[rows(x, near(i)), :], GW + i - 1, dev_z[i])
+    mine = cb.at[pl.ds(pl.multiple_of(x * 64, 64), 64), :]
+    send(mine, mine, GW + 3, dev_x)
+    for i in (0,) + ORDER:
+        ref = blk(X, y, c, xn, near(i))
+        arrive(ref, GT + 3 + i, dev_x)
+        send(ref, ref, GT + 11 + i, dev_y)
+        sib(TOKS, 0, 1, i)
+        ref = blk(Y, yn, c, x, near(i))
+        arrive(ref, GC + 3 + i, dev_y)
+        send(ref, ref, GC + 11 + i, dev_x)
+        sib(COTS, 1, 0, i)
+
+    gacc[...] = jnp.zeros_like(gacc)
+    uacc[...] = jnp.zeros_like(uacc)
+    bacc[...] = jnp.zeros_like(bacc)
+
+    def project(hh):
+        at = pl.ds(pl.multiple_of(hh * cols, cols), cols)
+        for j in range(2):
+            own = slice(j * units, (j + 1) * units)
+            gacc[:, own] += jnp.dot(X[hh], wg[j, at, :], preferred_element_type=F32)
+            uacc[:, own] += jnp.dot(X[hh], wu[j, at, :], preferred_element_type=F32)
+
+    wcopies[0].wait()
+    wcopies[1].wait()
+    for xo in range(2):
+        for i in range(4):
+            sib_arrive(TOKS, 0, xo, i)
+    lax.fori_loop(0, 2, lambda k, _: (project(y * 2 + k), 0)[1], 0)
+
+    for a in range(2):
+        for i in (0,) + ORDER:
+            arrive(blk(X, yn, c, (x, xn)[a], near(i)), GT + 7 + 4 * a + i, dev_y)
+            sib(TOKS, 1, a, i)
+            arrive(blk(Y, (y, yn)[a], c, xn, near(i)), GC + 7 + 4 * a + i, dev_x)
+            sib(COTS, a, 1, i)
+    for xo in range(2):
+        for i in range(4):
+            sib_arrive(TOKS, 1, xo, i)
+    lax.fori_loop(0, 2, lambda k, _: (project(yn * 2 + k), 0)[1], 0)
+    for copy in wcopies[2:]:
+        copy.wait()
+    for yo in range(2):
+        for xo in range(2):
+            for i in range(4):
+                sib_arrive(COTS, yo, xo, i)
+
+    def back(hh, _):
+        bacc[...] += dot_nt(Y[hh], wd[hh])
+        return 0
+
+    lax.fori_loop(0, 4, back, 0)
+    other = cb.at[pl.ds(pl.multiple_of(xn * 64, 64), 64), :]
+    arrive(other, GW + 3, dev_x)
+    wide = lax.broadcasted_iota(jnp.int32, (8 * ROWS, 128), 1)
+    weights = cb[...].astype(F32)
+    for j in range(2):
+        own = slice(j * units, (j + 1) * units)
+        mark = e * 2 + j
+        scale = jnp.sum(
+            jnp.where((wide == mark) | (wide == mark + 16), weights, 0.0), axis=1, keepdims=True
+        )
+        g, u, b = gacc[:, own], uacc[:, own], bacc[:, own] * scale
+        s = jax.nn.sigmoid(g)
+        act = g * s
+        H[:, own] = (act * u * scale).astype(BF16)
+        G[:, own] = (b * u * s * (1.0 + g * (1.0 - s))).astype(BF16)
+        G[:, (2 + j) * units : (3 + j) * units] = (b * act).astype(BF16)
+
+    def out_chunk(hh):
+        for n in range(cols // 256):
+            at = slice(n * 256, (n + 1) * 256)
+            PO[hh, :, at] = jnp.dot(H[...], wd[hh, :, at], preferred_element_type=F32).astype(BF16)
+
+    def grad_chunk(hh):
+        for n in range(cols // 256):
+            at = pl.ds(pl.multiple_of(hh * cols + n * 256, 256), 256)
+            total = dot_nt(G[:, :units], wg[0, at, :])
+            total += dot_nt(G[:, units : 2 * units], wg[1, at, :])
+            total += dot_nt(G[:, 2 * units : 3 * units], wu[0, at, :])
+            total += dot_nt(G[:, 3 * units :], wu[1, at, :])
+            PG[hh, :, n * 256 : (n + 1) * 256] = total.astype(BF16)
+
+    def to(i):
+        return (z + i) % 4
+
+    def add(acc, yy, xx, zz, terms):
+        at = (yy * 2 + c, rows(xx, zz), slice(None))
+        total = acc[at].astype(F32)
+        for term in terms:
+            total = total + term.astype(F32)
+        return at, total
+
+    FAR = ORDER + (0,)
+
+    def core_send(acc, rc, base, yo):
+        yy = (y, yn)[yo]
+        send(acc.at[yy * 2 + cn], rc.at[yy], base + yo, dev_s)
+
+    out_chunk(yn * 2 + cn)
+    core_send(PO, RcO, RO, 1)
+    out_chunk(yn * 2 + c)
+    grad_chunk(yn * 2 + cn)
+    core_send(PG, RcG, RG, 1)
+    arrive(RcO.at[yn], RO + 1, dev_s)
+    for a in (1, 0):
+        for i in FAR:
+            xx, zz = (x, xn)[a], to(i)
+            at, total = add(PO, yn, xx, zz, [RcO[yn, rows(xx, zz), :]])
+            PO[at] = total.astype(BF16)
+            send(PO.at[at], RyO.at[rows(xx, zz), :], RO + 2 + 4 * a + i, dev_y)
+    grad_chunk(yn * 2 + c)
+    arrive(RcG.at[yn], RG + 1, dev_s)
+    for i in FAR:
+        at, total = add(PG, yn, xn, to(i), [RcG[yn, rows(xn, to(i)), :]])
+        PG[at] = total.astype(BF16)
+        send(PG.at[at], RxG.at[yn, half(to(i)), :], RG + 6 + i, dev_x)
+    grad_chunk(y * 2 + cn)
+    core_send(PG, RcG, RG, 0)
+    grad_chunk(y * 2 + c)
+    out_chunk(y * 2 + cn)
+    core_send(PO, RcO, RO, 0)
+    arrive(RcG.at[y], RG, dev_s)
+    for i in FAR:
+        at, total = add(PG, y, xn, to(i), [RcG[y, rows(xn, to(i)), :]])
+        PG[at] = total.astype(BF16)
+        send(PG.at[at], RxG.at[y, half(to(i)), :], RG + 2 + i, dev_x)
+    out_chunk(y * 2 + c)
+    arrive(RcO.at[y], RO, dev_s)
+    for i in FAR:
+        zz = to(i)
+        arrive(RyO.at[rows(xn, zz), :], RO + 6 + i, dev_y)
+        at, total = add(PO, y, xn, zz, [RcO[y, rows(xn, zz), :], RyO[rows(xn, zz), :]])
+        PO[at] = total.astype(BF16)
+        send(PO.at[at], RxO.at[half(zz), :], RO + 10 + i, dev_x)
+        arrive(RxG.at[yn, half(zz), :], RG + 6 + i, dev_x)
+        at, total = add(PG, yn, x, zz, [RcG[yn, rows(x, zz), :], RxG[yn, half(zz), :]])
+        PG[at] = total.astype(BF16)
+        send(PG.at[at], RyG.at[half(zz), :], RG + 10 + i, dev_y)
+    for i in FAR:
+        zz = to(i)
+        for acc, rc, base, d1, d2, one, two, rz, res in (
+            (PO, RcO, RO, dev_y, dev_x, RyO.at[rows(x, zz), :], RxO.at[half(zz), :], RzO, out),
+            (PG, RcG, RG, dev_x, dev_y, RxG.at[y, half(zz), :], RyG.at[half(zz), :], RzG, grad),
+        ):
+            arrive(one, base + 2 + i, d1)
+            arrive(two, base + 10 + i, d2)
+            at, total = add(acc, y, x, zz, [rc[y, rows(x, zz), :], one[...], two[...]])
+            if i:
+                acc[at] = total.astype(BF16)
+                send(acc.at[at], rz.at[i - 1], base + 14 + i - 1, dev_z[i])
+            else:
+                for k in ORDER:
+                    arrive(rz.at[k - 1], base + 14 + k - 1, dev_z[k])
+                    total = total + rz[k - 1].astype(F32)
+                res[...] = total.astype(BF16)
+    for copy in started:
+        copy.wait_send()
+
+
+def fused(tokens, routes, combine, w_gate, w_up, w_down, cotangent):
+    cols = tokens.shape[1]
+    units = w_gate.shape[2]
+    width = w_gate.shape[1]
+    all_rows = 8 * ROWS
+    vmem = pl.BlockSpec(memory_space=pltpu.VMEM)
+    hbm = pl.BlockSpec(memory_space=pl.ANY)
+    bf = lambda *shape: pltpu.VMEM(shape, BF16)
+    fl = lambda *shape: pltpu.VMEM(shape, F32)
+    flops = 2 * all_rows * 6 * 2 * units * width
+    return pl.pallas_call(
+        kernel,
+        out_shape=(
+            jax.ShapeDtypeStruct(tokens.shape, BF16),
+            jax.ShapeDtypeStruct(tokens.shape, BF16),
+        ),
+        in_specs=[vmem] * 4 + [hbm] * 3,
+        out_specs=(vmem, vmem),
+        scratch_shapes=[
+            bf(4, all_rows, cols), bf(4, all_rows, cols),
+            bf(2, width, units), bf(2, width, units), bf(4, 2 * units, cols),
+            bf(all_rows, 128),
+            fl(all_rows, 2 * units), fl(all_rows, 2 * units), fl(all_rows, 2 * units),
+            bf(all_rows, 2 * units), bf(all_rows, 4 * units),
+            bf(4, all_rows, cols), bf(4, all_rows, cols),
+            bf(2, all_rows, cols), bf(2, all_rows, cols),
+            bf(all_rows, cols), bf(4 * ROWS, cols), bf(3, ROWS, cols),
+            bf(2, 4 * ROWS, cols), bf(4 * ROWS, cols), bf(3, ROWS, cols),
+            pltpu.SemaphoreType.DMA((COPIES,)),
+            pltpu.SemaphoreType.DMA((COPIES,)),
+            pltpu.SemaphoreType.DMA((10,)),
+        ],
+        compiler_params=pltpu.CompilerParams(
+            collective_id=0, has_side_effects=True, vmem_limit_bytes=52 * 2**20
+        ),
+        cost_estimate=pl.CostEstimate(
+            flops=flops, bytes_accessed=2 * 3 * 2 * units * width, transcendentals=0
+        ),
+    )(tokens, cotangent, routes, combine, w_gate, w_up, w_down)
+
+
 def solution(mesh):
+    small = mesh.shape["expert"] == 8 and mesh.shape["hidden"] == 4
     return jax.shard_map(
-        per_device,
+        fused if small else per_device,
         mesh=mesh,
-        in_specs=(
-            P("expert", "hidden"),
-            P("expert", None),
-            P("expert", None),
-            P("expert", None, "hidden"),
-            P("expert", None, "hidden"),
-            P("expert", "hidden", None),
-            P("expert", "hidden"),
-        ),
+        in_specs=SPECS,
         out_specs=(P("expert", "hidden"), P("expert", "hidden")),
         check_vma=False,
     )

time: 347 us -> 67.1 us (0.19)
  waiting for transfers between devices: 238 us -> 0 us
  Pallas kernels: 0 us -> 61.8 us
  matrix products: 33.6 us -> 0 us
  starting transfers between devices: 21.8 us -> 0 us
  local copies, waits for them, and re-layouts: 22.7 us -> 4.4 us
  between operations: 14.2 us -> 0.64 us
  blocking collectives: 13 us -> 0 us
    all_to_all x4 -> x0, waiting for transfers between devices: 167 us -> none  [the longest x1 73.2 us: per_device(): lax.all_to_all(pack_rows(full_grads), 'expert', split_axis=0, concat_axis...]
    reduce_scatter x2 -> x0, waiting for transfers between devices: 70.6 us -> none  [the longest x1 36.3 us: per_device(): lax.psum_scatter(out_terms, 'hidden', scatter_dimension=2, tiled=True)]
    pallas_call x0 -> x1, Pallas kernels: none -> 61.8 us  [fused(): pl.pallas_call(kernel, out_shape=(jax.ShapeDtypeStruct(tokens.shape, BF16...]
    dot_general x6 -> x0, matrix products: 33.6 us -> none  [the longest x1 8.67 us: per_device(): jnp.einsum('erf,edf->erd', grad_gate, w_gate, preferred_element_type=jnp....]
    all_to_all x4 -> x0, starting transfers between devices: 21.5 us -> none  [the longest x1 6.04 us: per_device(): lax.all_to_all(pack_rows(full_tokens), 'expert', split_axis=0, concat_axi...]
    all_gather x2 -> x0, blocking collectives: 13 us -> none  [the longest x1 7.26 us: per_device(): lax.all_gather(tokens, 'hidden', axis=1, tiled=True)]
    gather x4 -> x0, local copies, waits for them, and re-layouts: 11.3 us -> none  [the longest x2 9.48 us: pack_rows(): return padded[source_rows].reshape(experts, capacity, values.shape[1])]
    transpose x2 -> x0, local copies, waits for them, and re-layouts: 4.83 us -> none  [to_local(): arrived.reshape(sources, local_experts, capacity, columns)]
  transfers between devices with their start and end apart: 6 -> 0, of which waited for: 5 -> 0; matrix products, arithmetic and copies ran while one was open for 7% -> 0% of each run, Pallas kernels for 0% -> 0%
where the time goes in v1:
time: 67.1 us; the launch traced here: 66.8 us
  Pallas kernels  61.8 us (92%)
  local copies, waits for them, and re-layouts  4.4 us (7%)
    pallas_call x1, Pallas kernels, fused(): pl.pallas_call(kernel, out_shape=(jax.ShapeDtypeStruct(tokens.shape, BF16...  61.8 us
    unnamed x8, local copies, waits for them, and re-layouts  4.4 us

profile of v1, /device:TPU:0, one launch (start us, length us, event | category | flops | bytes accessed | tf_op | source)
XLA Modules:
  0.0 66.8 jit_solution(14167019210555674227)
XLA Ops:
  0.6 0.8 %copy.9.routes = s32[16,8]{1,0:T(8,128)S(1)} copy(s32[16,8]{0,1:T(8,128)} %param.8) | data formatting | bytes 1024 | tf_op args[1]
  1.4 0.8 %copy.10.comb = f32[16,8]{1,0:T(8,128)S(1)} copy(f32[16,8]{0,1:T(8,128)} %param.9) | data formatting | bytes 1024 | tf_op args[2]
  2.1 0.0 copy-start
  2.1 0.8 %copy-done = bf16[16,1792]{1,0:T(8,128)(2,1)S(1)} copy-done((bf16[16,1792]{1,0:T(8,128)(2,1)S(1)}, bf16[16,1792]{1,0:T(8,128)(2,1)}, u32[]{:S(2)}) %copy-start) | copy-done | bytes 57368
  3.0 0.0 copy-start.1
  3.0 0.8 %copy-done.1 = bf16[16,1792]{1,0:T(8,128)(2,1)S(1)} copy-done((bf16[16,1792]{1,0:T(8,128)(2,1)S(1)}, bf16[16,1792]{1,0:T(8,128)(2,1)}, u32[]{:S(2)}) %copy-start.1) | copy-done | bytes 57368
  3.8 61.8 %shard_map.86 = (bf16[16,1792]{1,0:T(8,128)(2,1)S(1)}, bf16[16,1792]{1,0:T(8,128)(2,1)S(1)}) custom-call(bf16[16,1792]{1,0:T(8,128)(2,1)S(1)} %copy-done, bf16[16,1792]{1,0:T(8,128)(2,1)S(1)} %copy-done.1, s32[16,8]{1,0:T(8,128)S(1)} %copy.9.routes, f32[16,8]{1,0:T(8,128)S(1)} %copy.10.comb, bf16[2,7168,256]{2,1,0:T(8,128)(2,1)} %wg_hbm.1, ...), custom_call_target="tpu_custom_call" | custom-call | flops 5637144576 | bytes 22020096 | tf_op jit(solution)/shard_map/pallas_call | solution.py:397
  65.6 0.6 copy.13
  66.2 0.6 copy.14
Async XLA Ops:
  2.1 0.8 %copy-start = (bf16[16,1792]{1,0:T(8,128)(2,1)S(1)}, bf16[16,1792]{1,0:T(8,128)(2,1)}, u32[]{:S(2)}) copy-start(bf16[16,1792]{1,0:T(8,128)(2,1)} %tok.1) | copy-start | bytes 172036
  3.0 0.8 %copy-start.1 = (bf16[16,1792]{1,0:T(8,128)(2,1)S(1)}, bf16[16,1792]{1,0:T(8,128)(2,1)}, u32[]{:S(2)}) copy-start(bf16[16,1792]{1,0:T(8,128)(2,1)} %cot.1) | copy-start | bytes 172036

commit v2 on v1

--- a/solution.py
+++ b/solution.py
@@ -117,7 +117,7 @@
 def kernel(
     tok, cot, routes, comb, wg_hbm, wu_hbm, wd_hbm, out, grad,
     X, Y, wg, wu, wd, cb, gacc, uacc, bacc, H, G,
-    PO, PG, RcO, RcG, RyO, RxO, RzO, RxG, RyG, RzG, ssem, rsem, lsem,
+    PO, PG, RcO, RcG, R1O, R2O, RzO, R1G, R2G, RzG, ssem, rsem, lsem,
 ):
     e, h = lax.axis_index("expert"), lax.axis_index("hidden")
     z, x, y, c = e // 2, e % 2, h // 2, h % 2
@@ -125,13 +125,13 @@
     cols = tok.shape[1]
     units = wd_hbm.shape[1]
     dev_x, dev_y, dev_s = (z * 2 + xn, h), (e, yn * 2 + c), (e, y * 2 + cn)
+    xf, yf = c * x + (1 - c) * xn, c * yn + (1 - c) * y
+    xs, ys = c * xn + (1 - c) * x, c * y + (1 - c) * yn
+    dev_1, dev_2 = (z * 2 + xf, yf * 2 + c), (z * 2 + xs, ys * 2 + c)
     dev_z = {i: (((z + i) % 4) * 2 + x, h) for i in ORDER}
 
     def rows(xx, zz):
         return pl.ds(pl.multiple_of((xx * 4 + zz) * ROWS, ROWS), ROWS)
-
-    def half(zz):
-        return pl.ds(pl.multiple_of(zz * ROWS, ROWS), ROWS)
 
     started = []
 
@@ -169,37 +169,56 @@
     def near(i):
         return (z - i) % 4
 
-    def blk(buf, yy, cc, xx, zz):
-        return buf.at[yy * 2 + cc, rows(xx, zz), :]
-
-    def first(arr, i):
-        buf, base, dev1, dev2 = arr
-        ref = blk(buf, y, c, x, near(i))
-        send(ref, ref, base + 3 + i, dev1)
-        send(ref, ref, base + 7 + i, dev2)
-
-    def sib(arr, yo, xo, i):
-        ref = blk(arr[0], (y, yn)[yo], c, (x, xn)[xo], near(i))
-        send(ref, ref, arr[1] + 15 + 8 * yo + 4 * xo + i, dev_s)
-
-    def sib_arrive(arr, yo, xo, i):
-        ref = blk(arr[0], (y, yn)[yo], cn, (x, xn)[xo], near(i))
-        arrive(ref, arr[1] + 15 + 8 * yo + 4 * xo + i, dev_s)
-
-    TOKS, COTS = (X, GT, dev_x, dev_y), (Y, GC, dev_y, dev_x)
-    BOTH = (TOKS, COTS)
+    def blk(buf, yy, cc, xx, i):
+        return buf.at[yy * 2 + cc, rows(xx, near(i)), :]
+
+    KINDS = ((y, x), (yf, xf), (ys, xs), (yn, xn))
+    SIBS = ((y, x), (ys, xs), (yf, xf), (yn, xn))
+    TOKS, COTS = (X, GT), (Y, GC)
+    ALL = (0,) + ORDER
+
+    def sib(arr, kind, i):
+        ref = blk(arr[0], KINDS[kind][0], c, KINDS[kind][1], i)
+        send(ref, ref, arr[1] + 15 + 4 * kind + i, dev_s)
+
+    def sib_all(arr):
+        for kind in range(4):
+            for i in range(4):
+                ref = blk(arr[0], SIBS[kind][0], cn, SIBS[kind][1], i)
+                arrive(ref, arr[1] + 15 + 4 * kind + i, dev_s)
+
+    def z_send(arr, i):
+        ref = blk(arr[0], y, c, x, 0)
+        send(ref, ref, arr[1] + i - 1, dev_z[i])
+
+    def spread(arr, i):
+        ref = blk(arr[0], y, c, x, i)
+        if i:
+            arrive(ref, arr[1] + i - 1, dev_z[i])
+        send(ref, ref, arr[1] + 7 + i, dev_2)
+        send(ref, ref, arr[1] + 3 + i, dev_1)
+        sib(arr, 0, i)
+
+    def from_first(arr, i):
+        ref = blk(arr[0], yf, c, xf, i)
+        arrive(ref, arr[1] + 3 + i, dev_1)
+        send(ref, ref, arr[1] + 11 + i, dev_2)
+        sib(arr, 1, i)
+
+    def from_second(arr, a, i):
+        ref = blk(arr[0], (ys, yn)[a], c, (xs, xn)[a], i)
+        arrive(ref, arr[1] + 7 + 4 * a + i, dev_2)
+        sib(arr, 2 + a, i)
+
     for i in ORDER:
-        for arr in BOTH:
-            ref = blk(arr[0], y, c, x, z)
-            send(ref, ref, arr[1] + i - 1, dev_z[i])
+        z_send(TOKS, i)
         if i == ORDER[0]:
-            for arr in BOTH:
-                first(arr, 0)
+            spread(TOKS, 0)
     for i in ORDER:
         ref = cb.at[rows(x, z), :]
         send(ref, ref, GW + i - 1, dev_z[i])
-    for arr in BOTH:
-        sib(arr, 0, 0, 0)
+    for i in ORDER:
+        z_send(COTS, i)
 
     wcopies = [
         pltpu.make_async_copy(wg_hbm, wg, lsem.at[0]),
@@ -217,81 +236,57 @@
     for copy in wcopies:
         copy.start()
 
+    gacc[...] = jnp.zeros_like(gacc)
+    uacc[...] = jnp.zeros_like(uacc)
+    bacc[...] = jnp.zeros_like(bacc)
     for i in ORDER:
-        for arr in BOTH:
-            arrive(blk(arr[0], y, c, x, near(i)), arr[1] + i - 1, dev_z[i])
-            first(arr, i)
-            sib(arr, 0, 0, i)
+        spread(TOKS, i)
+    for i in ALL:
+        from_first(TOKS, i)
+    spread(COTS, 0)
     for i in ORDER:
         arrive(cb.at[rows(x, near(i)), :], GW + i - 1, dev_z[i])
     mine = cb.at[pl.ds(pl.multiple_of(x * 64, 64), 64), :]
     send(mine, mine, GW + 3, dev_x)
-    for i in (0,) + ORDER:
-        ref = blk(X, y, c, xn, near(i))
-        arrive(ref, GT + 3 + i, dev_x)
-        send(ref, ref, GT + 11 + i, dev_y)
-        sib(TOKS, 0, 1, i)
-        ref = blk(Y, yn, c, x, near(i))
-        arrive(ref, GC + 3 + i, dev_y)
-        send(ref, ref, GC + 11 + i, dev_x)
-        sib(COTS, 1, 0, i)
-
-    gacc[...] = jnp.zeros_like(gacc)
-    uacc[...] = jnp.zeros_like(uacc)
-    bacc[...] = jnp.zeros_like(bacc)
-
-    def project(hh):
+    for i in ALL:
+        if i:
+            spread(COTS, i)
+        from_second(TOKS, 0, i)
+    for i in ALL:
+        from_second(TOKS, 1, i)
+
+    def project(hh, _):
         at = pl.ds(pl.multiple_of(hh * cols, cols), cols)
         for j in range(2):
             own = slice(j * units, (j + 1) * units)
             gacc[:, own] += jnp.dot(X[hh], wg[j, at, :], preferred_element_type=F32)
             uacc[:, own] += jnp.dot(X[hh], wu[j, at, :], preferred_element_type=F32)
+        return 0
 
     wcopies[0].wait()
     wcopies[1].wait()
-    for xo in range(2):
-        for i in range(4):
-            sib_arrive(TOKS, 0, xo, i)
-    lax.fori_loop(0, 2, lambda k, _: (project(y * 2 + k), 0)[1], 0)
-
-    for a in range(2):
-        for i in (0,) + ORDER:
-            arrive(blk(X, yn, c, (x, xn)[a], near(i)), GT + 7 + 4 * a + i, dev_y)
-            sib(TOKS, 1, a, i)
-            arrive(blk(Y, (y, yn)[a], c, xn, near(i)), GC + 7 + 4 * a + i, dev_x)
-            sib(COTS, a, 1, i)
-    for xo in range(2):
-        for i in range(4):
-            sib_arrive(TOKS, 1, xo, i)
-    lax.fori_loop(0, 2, lambda k, _: (project(yn * 2 + k), 0)[1], 0)
-    for copy in wcopies[2:]:
-        copy.wait()
-    for yo in range(2):
-        for xo in range(2):
-            for i in range(4):
-                sib_arrive(COTS, yo, xo, i)
-
-    def back(hh, _):
-        bacc[...] += dot_nt(Y[hh], wd[hh])
-        return 0
-
-    lax.fori_loop(0, 4, back, 0)
+    sib_all(TOKS)
+    lax.fori_loop(0, 2, project, 0)
+    for i in ALL:
+        from_first(COTS, i)
+    lax.fori_loop(2, 4, project, 0)
+
     other = cb.at[pl.ds(pl.multiple_of(xn * 64, 64), 64), :]
     arrive(other, GW + 3, dev_x)
     wide = lax.broadcasted_iota(jnp.int32, (8 * ROWS, 128), 1)
     weights = cb[...].astype(F32)
+    scales = []
     for j in range(2):
         own = slice(j * units, (j + 1) * units)
         mark = e * 2 + j
         scale = jnp.sum(
             jnp.where((wide == mark) | (wide == mark + 16), weights, 0.0), axis=1, keepdims=True
         )
-        g, u, b = gacc[:, own], uacc[:, own], bacc[:, own] * scale
-        s = jax.nn.sigmoid(g)
-        act = g * s
-        H[:, own] = (act * u * scale).astype(BF16)
-        G[:, own] = (b * u * s * (1.0 + g * (1.0 - s))).astype(BF16)
-        G[:, (2 + j) * units : (3 + j) * units] = (b * act).astype(BF16)
+        scales.append(scale)
+        g, u = gacc[:, own], uacc[:, own]
+        H[:, own] = (g * jax.nn.sigmoid(g) * u * scale).astype(BF16)
+    for copy in wcopies[2:]:
+        copy.wait()
 
     def out_chunk(hh):
         for n in range(cols // 256):
@@ -310,76 +305,96 @@
     def to(i):
         return (z + i) % 4
 
-    def add(acc, yy, xx, zz, terms):
-        at = (yy * 2 + c, rows(xx, zz), slice(None))
-        total = acc[at].astype(F32)
+    FAR = ORDER + (0,)
+    OUTS, GRADS = (PO, RcO, R1O, R2O, RzO, RO, out), (PG, RcG, R1G, R2G, RzG, RG, grad)
+
+    def core_send(res, yo):
+        yy = (y, yn)[yo]
+        send(res[0].at[yy * 2 + cn], res[1].at[yy], res[5] + yo, dev_s)
+
+    def core_arrive(res, yo):
+        arrive(res[1].at[(y, yn)[yo]], res[5] + yo, dev_s)
+
+    def add(res, yy, xx, i, terms):
+        at = (yy * 2 + c, rows(xx, to(i)), slice(None))
+        total = res[0][at].astype(F32) + res[1][yy, rows(xx, to(i)), :].astype(F32)
         for term in terms:
             total = total + term.astype(F32)
         return at, total
 
-    FAR = ORDER + (0,)
-
-    def core_send(acc, rc, base, yo):
-        yy = (y, yn)[yo]
-        send(acc.at[yy * 2 + cn], rc.at[yy], base + yo, dev_s)
+    def first_sum(res, a):
+        for i in FAR:
+            at, total = add(res, (yn, yf)[a], (xn, xf)[a], i, [])
+            res[0][at] = total.astype(BF16)
+            send(res[0].at[at], res[2].at[a, i], res[5] + 2 + 4 * a + i, dev_1)
+
+    def second_sum(res):
+        for i in FAR:
+            arrive(res[2].at[0, i], res[5] + 2 + i, dev_1)
+            at, total = add(res, ys, xs, i, [res[2][0, i]])
+            res[0][at] = total.astype(BF16)
+            send(res[0].at[at], res[3].at[i], res[5] + 10 + i, dev_2)
+
+    def z_total(res, i):
+        arrive(res[2].at[1, i], res[5] + 6 + i, dev_1)
+        arrive(res[3].at[i], res[5] + 10 + i, dev_2)
+        return add(res, y, x, i, [res[2][1, i], res[3][i]])
+
+    def z_sum(res):
+        for i in ORDER:
+            at, total = z_total(res, i)
+            res[0][at] = total.astype(BF16)
+            send(res[0].at[at], res[4].at[i - 1], res[5] + 14 + i - 1, dev_z[i])
+
+    def last_sum(res):
+        _, total = z_total(res, 0)
+        for k in ORDER:
+            arrive(res[4].at[k - 1], res[5] + 14 + k - 1, dev_z[k])
+            total = total + res[4][k - 1].astype(F32)
+        res[6][...] = total.astype(BF16)
 
     out_chunk(yn * 2 + cn)
-    core_send(PO, RcO, RO, 1)
+    core_send(OUTS, 1)
     out_chunk(yn * 2 + c)
+    out_chunk(y * 2 + cn)
+    core_send(OUTS, 0)
+    core_arrive(OUTS, 1)
+    first_sum(OUTS, 0)
+    out_chunk(y * 2 + c)
+    core_arrive(OUTS, 0)
+    first_sum(OUTS, 1)
+    for a in range(2):
+        for i in ALL:
+            from_second(COTS, a, i)
+    sib_all(COTS)
+
+    def back(hh, _):
+        bacc[...] += dot_nt(Y[hh], wd[hh])
+        return 0
+
+    lax.fori_loop(0, 4, back, 0)
+    for j in range(2):
+        own = slice(j * units, (j + 1) * units)
+        g, u, b = gacc[:, own], uacc[:, own], bacc[:, own] * scales[j]
+        s = jax.nn.sigmoid(g)
+        G[:, own] = (b * u * s * (1.0 + g * (1.0 - s))).astype(BF16)
+        G[:, (2 + j) * units : (3 + j) * units] = (b * g * s).astype(BF16)
     grad_chunk(yn * 2 + cn)
-    core_send(PG, RcG, RG, 1)
-    arrive(RcO.at[yn], RO + 1, dev_s)
-    for a in (1, 0):
-        for i in FAR:
-            xx, zz = (x, xn)[a], to(i)
-            at, total = add(PO, yn, xx, zz, [RcO[yn, rows(xx, zz), :]])
-            PO[at] = total.astype(BF16)
-            send(PO.at[at], RyO.at[rows(xx, zz), :], RO + 2 + 4 * a + i, dev_y)
+    core_send(GRADS, 1)
+    second_sum(OUTS)
     grad_chunk(yn * 2 + c)
-    arrive(RcG.at[yn], RG + 1, dev_s)
-    for i in FAR:
-        at, total = add(PG, yn, xn, to(i), [RcG[yn, rows(xn, to(i)), :]])
-        PG[at] = total.astype(BF16)
-        send(PG.at[at], RxG.at[yn, half(to(i)), :], RG + 6 + i, dev_x)
+    core_arrive(GRADS, 1)
+    first_sum(GRADS, 0)
     grad_chunk(y * 2 + cn)
-    core_send(PG, RcG, RG, 0)
+    core_send(GRADS, 0)
     grad_chunk(y * 2 + c)
-    out_chunk(y * 2 + cn)
-    core_send(PO, RcO, RO, 0)
-    arrive(RcG.at[y], RG, dev_s)
-    for i in FAR:
-        at, total = add(PG, y, xn, to(i), [RcG[y, rows(xn, to(i)), :]])
-        PG[at] = total.astype(BF16)
-        send(PG.at[at], RxG.at[y, half(to(i)), :], RG + 2 + i, dev_x)
-    out_chunk(y * 2 + c)
-    arrive(RcO.at[y], RO, dev_s)
-    for i in FAR:
-        zz = to(i)
-        arrive(RyO.at[rows(xn, zz), :], RO + 6 + i, dev_y)
-        at, total = add(PO, y, xn, zz, [RcO[y, rows(xn, zz), :], RyO[rows(xn, zz), :]])
-        PO[at] = total.astype(BF16)
-        send(PO.at[at], RxO.at[half(zz), :], RO + 10 + i, dev_x)
-        arrive(RxG.at[yn, half(zz), :], RG + 6 + i, dev_x)
-        at, total = add(PG, yn, x, zz, [RcG[yn, rows(x, zz), :], RxG[yn, half(zz), :]])
-        PG[at] = total.astype(BF16)
-        send(PG.at[at], RyG.at[half(zz), :], RG + 10 + i, dev_y)
-    for i in FAR:
-        zz = to(i)
-        for acc, rc, base, d1, d2, one, two, rz, res in (
-            (PO, RcO, RO, dev_y, dev_x, RyO.at[rows(x, zz), :], RxO.at[half(zz), :], RzO, out),
-            (PG, RcG, RG, dev_x, dev_y, RxG.at[y, half(zz), :], RyG.at[half(zz), :], RzG, grad),
-        ):
-            arrive(one, base + 2 + i, d1)
-            arrive(two, base + 10 + i, d2)
-            at, total = add(acc, y, x, zz, [rc[y, rows(x, zz), :], one[...], two[...]])
-            if i:
-                acc[at] = total.astype(BF16)
-                send(acc.at[at], rz.at[i - 1], base + 14 + i - 1, dev_z[i])
-            else:
-                for k in ORDER:
-                    arrive(rz.at[k - 1], base + 14 + k - 1, dev_z[k])
-                    total = total + rz[k - 1].astype(F32)
-                res[...] = total.astype(BF16)
+    core_arrive(GRADS, 0)
+    first_sum(GRADS, 1)
+    z_sum(OUTS)
+    second_sum(GRADS)
+    z_sum(GRADS)
+    last_sum(OUTS)
+    last_sum(GRADS)
     for copy in started:
         copy.wait_send()
 
@@ -410,8 +425,8 @@
             bf(all_rows, 2 * units), bf(all_rows, 4 * units),
             bf(4, all_rows, cols), bf(4, all_rows, cols),
             bf(2, all_rows, cols), bf(2, all_rows, cols),
-            bf(all_rows, cols), bf(4 * ROWS, cols), bf(3, ROWS, cols),
-            bf(2, 4 * ROWS, cols), bf(4 * ROWS, cols), bf(3, ROWS, cols),
+            bf(2, 4, ROWS, cols), bf(4, ROWS, cols), bf(3, ROWS, cols),
+            bf(2, 4, ROWS, cols), bf(4, ROWS, cols), bf(3, ROWS, cols),
             pltpu.SemaphoreType.DMA((COPIES,)),
             pltpu.SemaphoreType.DMA((COPIES,)),
             pltpu.SemaphoreType.DMA((10,)),

time: 67.1 us -> 58.1 us (0.87)
  Pallas kernels: 61.8 us -> 52.8 us
    pallas_call x1, Pallas kernels: 61.8 us -> 52.8 us  [fused(): pl.pallas_call(kernel, out_shape=(jax.ShapeDtypeStruct(tokens.shape, BF16...]
where the time goes in v2:
time: 58.1 us; the launch traced here: 57.9 us
  Pallas kernels  52.8 us (91%)
  local copies, waits for them, and re-layouts  4.4 us (8%)
  between operations  0.64 us (1%)
    pallas_call x1, Pallas kernels, fused(): pl.pallas_call(kernel, out_shape=(jax.ShapeDtypeStruct(tokens.shape, BF16...  52.8 us
    unnamed x8, local copies, waits for them, and re-layouts  4.4 us

profile of v2, /device:TPU:0, one launch (start us, length us, event | category | flops | bytes accessed | tf_op | source)
XLA Modules:
  0.0 57.9 jit_solution(17023648735202501312)
XLA Ops:
  0.6 0.8 %copy.9.routes = s32[16,8]{1,0:T(8,128)S(1)} copy(s32[16,8]{0,1:T(8,128)} %param.8) | data formatting | bytes 1024 | tf_op args[1]
  1.4 0.8 %copy.10.comb = f32[16,8]{1,0:T(8,128)S(1)} copy(f32[16,8]{0,1:T(8,128)} %param.9) | data formatting | bytes 1024 | tf_op args[2]
  2.1 0.0 copy-start
  2.1 0.8 %copy-done = bf16[16,1792]{1,0:T(8,128)(2,1)S(1)} copy-done((bf16[16,1792]{1,0:T(8,128)(2,1)S(1)}, bf16[16,1792]{1,0:T(8,128)(2,1)}, u32[]{:S(2)}) %copy-start) | copy-done | bytes 57368
  3.0 0.0 copy-start.1
  3.0 0.8 %copy-done.1 = bf16[16,1792]{1,0:T(8,128)(2,1)S(1)} copy-done((bf16[16,1792]{1,0:T(8,128)(2,1)S(1)}, bf16[16,1792]{1,0:T(8,128)(2,1)}, u32[]{:S(2)}) %copy-start.1) | copy-done | bytes 57368
  3.8 52.8 %shard_map.86 = (bf16[16,1792]{1,0:T(8,128)(2,1)S(1)}, bf16[16,1792]{1,0:T(8,128)(2,1)S(1)}) custom-call(bf16[16,1792]{1,0:T(8,128)(2,1)S(1)} %copy-done, bf16[16,1792]{1,0:T(8,128)(2,1)S(1)} %copy-done.1, s32[16,8]{1,0:T(8,128)S(1)} %copy.9.routes, f32[16,8]{1,0:T(8,128)S(1)} %copy.10.comb, bf16[2,7168,256]{2,1,0:T(8,128)(2,1)} %wg_hbm.1, ...), custom_call_target="tpu_custom_call" | custom-call | flops 5637144576 | bytes 22020096 | tf_op jit(solution)/shard_map/pallas_call | solution.py:412
  56.6 0.6 %copy.13 = bf16[16,1792]{1,0:T(8,128)(2,1)} copy(bf16[16,1792]{1,0:T(8,128)(2,1)S(1)} %get-tuple-element.4) | data formatting | bytes 114688
  57.2 0.6 %copy.14 = bf16[16,1792]{1,0:T(8,128)(2,1)} copy(bf16[16,1792]{1,0:T(8,128)(2,1)S(1)} %get-tuple-element.5) | data formatting | bytes 114688
Async XLA Ops:
  2.1 0.8 %copy-start = (bf16[16,1792]{1,0:T(8,128)(2,1)S(1)}, bf16[16,1792]{1,0:T(8,128)(2,1)}, u32[]{:S(2)}) copy-start(bf16[16,1792]{1,0:T(8,128)(2,1)} %tok.1) | copy-start | bytes 172036
  3.0 0.8 %copy-start.1 = (bf16[16,1792]{1,0:T(8,128)(2,1)S(1)}, bf16[16,1792]{1,0:T(8,128)(2,1)}, u32[]{:S(2)}) copy-start(bf16[16,1792]{1,0:T(8,128)(2,1)} %cot.1) | copy-start | bytes 172036

commit v3 on v2

--- a/solution.py
+++ b/solution.py
@@ -115,14 +115,14 @@
 
 
 def kernel(
-    tok, cot, routes, comb, wg_hbm, wu_hbm, wd_hbm, out, grad,
+    tok_hbm, cot_hbm, routes_hbm, comb_hbm, wg_hbm, wu_hbm, wd_hbm, out, grad,
     X, Y, wg, wu, wd, cb, gacc, uacc, bacc, H, G,
-    PO, PG, RcO, RcG, R1O, R2O, RzO, R1G, R2G, RzG, ssem, rsem, lsem,
+    PO, PG, RcO, RcG, R1O, R2O, RzO, R1G, R2G, RzG, ssem, rsem, lsem, routes, comb,
 ):
     e, h = lax.axis_index("expert"), lax.axis_index("hidden")
     z, x, y, c = e // 2, e % 2, h // 2, h % 2
     xn, yn, cn = 1 - x, 1 - y, 1 - c
-    cols = tok.shape[1]
+    cols = tok_hbm.shape[1]
     units = wd_hbm.shape[1]
     dev_x, dev_y, dev_s = (z * 2 + xn, h), (e, yn * 2 + c), (e, y * 2 + cn)
     xf, yf = c * x + (1 - c) * xn, c * yn + (1 - c) * y
@@ -154,16 +154,32 @@
     for dev in partners:
         pl.semaphore_signal(barrier, inc=1, device_id=dev, device_id_type=MESH)
 
-    X[h, rows(x, z), :] = tok[...]
-    Y[h, rows(x, z), :] = cot[...]
-    lane = lax.broadcasted_iota(jnp.int32, (ROWS, 128), 1)
-    expert = jnp.where(lane < 16, lane, lane - 16)
-    dense = jnp.zeros((ROWS, 128), F32)
-    for k in range(routes.shape[1]):
-        dense = dense + jnp.where(expert == routes[:, k : k + 1], comb[:, k : k + 1], 0.0)
-    high = dense.astype(BF16)
-    low = (dense - high.astype(F32)).astype(BF16)
-    cb[rows(x, z), :] = jnp.where(lane < 16, high.astype(F32), low.astype(F32)).astype(BF16)
+    own_in = [
+        pltpu.make_async_copy(routes_hbm, routes, lsem.at[10]),
+        pltpu.make_async_copy(comb_hbm, comb, lsem.at[11]),
+        pltpu.make_async_copy(tok_hbm, X.at[h, rows(x, z), :], lsem.at[12]),
+        pltpu.make_async_copy(cot_hbm, Y.at[h, rows(x, z), :], lsem.at[13]),
+    ]
+    for copy in own_in:
+        copy.start()
+    own_in[0].wait()
+    own_in[1].wait()
+    line = lax.broadcasted_iota(jnp.int32, (128, ROWS), 0)
+    expert = jnp.where(line < 16, line, line - 16)
+    dense = jnp.zeros((128, ROWS), F32)
+    for k in range(routes.shape[0]):
+        dense = dense + jnp.where(expert == routes[k : k + 1, :], comb[k : k + 1, :], 0.0)
+    high = dense.astype(BF16).astype(F32)
+    pair = jnp.where(line < 16, high, dense - high).astype(BF16)
+    unit = jnp.where(
+        lax.broadcasted_iota(jnp.int32, (ROWS, ROWS), 0)
+        == lax.broadcasted_iota(jnp.int32, (ROWS, ROWS), 1),
+        1.0,
+        0.0,
+    ).astype(BF16)
+    cb[rows(x, z), :] = dot_nt(unit, pair).astype(BF16)
+    own_in[2].wait()
+    own_in[3].wait()
     pl.semaphore_wait(barrier, len(partners))
 
     def near(i):
@@ -172,19 +188,19 @@
     def blk(buf, yy, cc, xx, i):
         return buf.at[yy * 2 + cc, rows(xx, near(i)), :]
 
-    KINDS = ((y, x), (yf, xf), (ys, xs), (yn, xn))
-    SIBS = ((y, x), (ys, xs), (yf, xf), (yn, xn))
-    TOKS, COTS = (X, GT), (Y, GC)
+    by_x, by_y, both_off = (y, xn), (yn, x), (yn, xn)
+    TOKS = (X, GT, ((y, x), by_x, by_y, both_off), dev_x, dev_y)
+    COTS = (Y, GC, ((y, x), by_y, by_x, both_off), dev_y, dev_x)
     ALL = (0,) + ORDER
 
     def sib(arr, kind, i):
-        ref = blk(arr[0], KINDS[kind][0], c, KINDS[kind][1], i)
+        ref = blk(arr[0], arr[2][kind][0], c, arr[2][kind][1], i)
         send(ref, ref, arr[1] + 15 + 4 * kind + i, dev_s)
 
-    def sib_all(arr):
-        for kind in range(4):
+    def sib_all(arr, kinds):
+        for kind in kinds:
             for i in range(4):
-                ref = blk(arr[0], SIBS[kind][0], cn, SIBS[kind][1], i)
+                ref = blk(arr[0], arr[2][kind][0], cn, arr[2][kind][1], i)
                 arrive(ref, arr[1] + 15 + 4 * kind + i, dev_s)
 
     def z_send(arr, i):
@@ -195,19 +211,19 @@
         ref = blk(arr[0], y, c, x, i)
         if i:
             arrive(ref, arr[1] + i - 1, dev_z[i])
-        send(ref, ref, arr[1] + 7 + i, dev_2)
-        send(ref, ref, arr[1] + 3 + i, dev_1)
+        send(ref, ref, arr[1] + 3 + i, arr[3])
+        send(ref, ref, arr[1] + 7 + i, arr[4])
         sib(arr, 0, i)
 
     def from_first(arr, i):
-        ref = blk(arr[0], yf, c, xf, i)
-        arrive(ref, arr[1] + 3 + i, dev_1)
-        send(ref, ref, arr[1] + 11 + i, dev_2)
+        ref = blk(arr[0], arr[2][1][0], c, arr[2][1][1], i)
+        arrive(ref, arr[1] + 3 + i, arr[3])
+        send(ref, ref, arr[1] + 11 + i, arr[4])
         sib(arr, 1, i)
 
     def from_second(arr, a, i):
-        ref = blk(arr[0], (ys, yn)[a], c, (xs, xn)[a], i)
-        arrive(ref, arr[1] + 7 + 4 * a + i, dev_2)
+        ref = blk(arr[0], arr[2][2 + a][0], c, arr[2][2 + a][1], i)
+        arrive(ref, arr[1] + 7 + 4 * a + i, arr[4])
         sib(arr, 2 + a, i)
 
     for i in ORDER:
@@ -241,35 +257,38 @@
     bacc[...] = jnp.zeros_like(bacc)
     for i in ORDER:
         spread(TOKS, i)
+    spread(COTS, 0)
     for i in ALL:
         from_first(TOKS, i)
-    spread(COTS, 0)
-    for i in ORDER:
-        arrive(cb.at[rows(x, near(i)), :], GW + i - 1, dev_z[i])
-    mine = cb.at[pl.ds(pl.multiple_of(x * 64, 64), 64), :]
-    send(mine, mine, GW + 3, dev_x)
-    for i in ALL:
-        if i:
-            spread(COTS, i)
-        from_second(TOKS, 0, i)
-    for i in ALL:
-        from_second(TOKS, 1, i)
-
-    def project(hh, _):
+
+    def project(hh):
         at = pl.ds(pl.multiple_of(hh * cols, cols), cols)
         for j in range(2):
             own = slice(j * units, (j + 1) * units)
             gacc[:, own] += jnp.dot(X[hh], wg[j, at, :], preferred_element_type=F32)
             uacc[:, own] += jnp.dot(X[hh], wu[j, at, :], preferred_element_type=F32)
-        return 0
 
     wcopies[0].wait()
     wcopies[1].wait()
-    sib_all(TOKS)
-    lax.fori_loop(0, 2, project, 0)
+    project(y * 2 + c)
+    for i in ORDER:
+        arrive(cb.at[rows(x, near(i)), :], GW + i - 1, dev_z[i])
+    mine = cb.at[pl.ds(pl.multiple_of(x * 64, 64), 64), :]
+    send(mine, mine, GW + 3, dev_x)
+    for i in ORDER:
+        spread(COTS, i)
+    for i in ALL:
+        from_second(TOKS, 0, i)
+    sib_all(TOKS, (0, 1))
+    project(y * 2 + cn)
     for i in ALL:
         from_first(COTS, i)
-    lax.fori_loop(2, 4, project, 0)
+        from_second(TOKS, 1, i)
+    project(yn * 2 + c)
+    for i in ALL:
+        from_second(COTS, 0, i)
+    sib_all(TOKS, (2, 3))
+    project(yn * 2 + cn)
 
     other = cb.at[pl.ds(pl.multiple_of(xn * 64, 64), 64), :]
     arrive(other, GW + 3, dev_x)
@@ -363,10 +382,9 @@
     out_chunk(y * 2 + c)
     core_arrive(OUTS, 0)
     first_sum(OUTS, 1)
-    for a in range(2):
-        for i in ALL:
-            from_second(COTS, a, i)
-    sib_all(COTS)
+    for i in ALL:
+        from_second(COTS, 1, i)
+    sib_all(COTS, range(4))
 
     def back(hh, _):
         bacc[...] += dot_nt(Y[hh], wd[hh])
@@ -405,7 +423,7 @@
     width = w_gate.shape[1]
     all_rows = 8 * ROWS
     vmem = pl.BlockSpec(memory_space=pltpu.VMEM)
-    hbm = pl.BlockSpec(memory_space=pl.ANY)
+    hbm = pl.BlockSpec(memory_space=pltpu.HBM)
     bf = lambda *shape: pltpu.VMEM(shape, BF16)
     fl = lambda *shape: pltpu.VMEM(shape, F32)
     flops = 2 * all_rows * 6 * 2 * units * width
@@ -415,7 +433,7 @@
             jax.ShapeDtypeStruct(tokens.shape, BF16),
             jax.ShapeDtypeStruct(tokens.shape, BF16),
         ),
-        in_specs=[vmem] * 4 + [hbm] * 3,
+        in_specs=[hbm] * 7,
         out_specs=(vmem, vmem),
         scratch_shapes=[
             bf(4, all_rows, cols), bf(4, all_rows, cols),
@@ -429,15 +447,17 @@
             bf(2, 4, ROWS, cols), bf(4, ROWS, cols), bf(3, ROWS, cols),
             pltpu.SemaphoreType.DMA((COPIES,)),
             pltpu.SemaphoreType.DMA((COPIES,)),
-            pltpu.SemaphoreType.DMA((10,)),
+            pltpu.SemaphoreType.DMA((14,)),
+            pltpu.VMEM(routes.shape[::-1], jnp.int32),
+            fl(*routes.shape[::-1]),
         ],
         compiler_params=pltpu.CompilerParams(
-            collective_id=0, has_side_effects=True, vmem_limit_bytes=52 * 2**20
+            collective_id=0, has_side_effects=True, vmem_limit_bytes=64 * 2**20
         ),
         cost_estimate=pl.CostEstimate(
             flops=flops, bytes_accessed=2 * 3 * 2 * units * width, transcendentals=0
         ),
-    )(tokens, cotangent, routes, combine, w_gate, w_up, w_down)
+    )(tokens, cotangent, routes.T, combine.T, w_gate, w_up, w_down)
 
 
 def solution(mesh):

time: 58.1 us -> 57.8 us (level)
  local copies, waits for them, and re-layouts: 4.4 us -> 2.89 us
  Pallas kernels: 52.8 us -> 54 us
    unnamed x8 -> x2, local copies, waits for them, and re-layouts: 4.4 us -> 2.89 us
    pallas_call x1, Pallas kernels: 52.8 us -> 54 us  [fused(): pl.pallas_call(kernel, out_shape=(jax.ShapeDtypeStruct(tokens.shape, BF16...]
where the time goes in v3:
time: 57.8 us; the launch traced here: 57.5 us
  Pallas kernels  54 us (93%)
  local copies, waits for them, and re-layouts  2.89 us (5%)
  between operations  0.64 us (1%)
    pallas_call x1, Pallas kernels, fused(): pl.pallas_call(kernel, out_shape=(jax.ShapeDtypeStruct(tokens.shape, BF16...  54 us
    unnamed x2, local copies, waits for them, and re-layouts  2.89 us

profile of v3, /device:TPU:0, one launch (start us, length us, event | category | flops | bytes accessed | tf_op | source)
XLA Modules:
  0.0 57.5 jit_solution(8127756683395511334)
XLA Ops:
  0.6 54.0 %shard_map.86 = (bf16[16,1792]{1,0:T(8,128)(2,1)}, bf16[16,1792]{1,0:T(8,128)(2,1)}) custom-call(bf16[16,1792]{1,0:T(8,128)(2,1)} %tok_hbm.1, bf16[16,1792]{1,0:T(8,128)(2,1)} %cot_hbm.1, s32[8,16]{1,0:T(8,128)} %bitcast.2, f32[8,16]{1,0:T(8,128)} %bitcast.3, bf16[2,7168,256]{2,1,0:T(8,128)(2,1)} %wg_hbm.1, bf16[2,7168,256]{2,1,0:T(8,128)(2,1)} %wu_hbm.1, ...), custom_call_target="tpu_custom_call" | custom-call | flops 5637144576 | bytes 22020096 | tf_op jit(solution)/shard_map/pallas_call | solution.py:430
  54.6 1.4 %copy.11 = bf16[16,1792]{1,0:T(8,128)(2,1)} copy(bf16[16,1792]{1,0:T(8,128)(2,1)} %get-tuple-element.4) | data formatting | bytes 114688
  56.1 1.4 %copy.12 = bf16[16,1792]{1,0:T(8,128)(2,1)} copy(bf16[16,1792]{1,0:T(8,128)(2,1)} %get-tuple-element.5) | data formatting | bytes 114688

commit v4 on v2

--- a/solution.py
+++ b/solution.py
@@ -115,14 +115,14 @@
 
 
 def kernel(
-    tok, cot, routes, comb, wg_hbm, wu_hbm, wd_hbm, out, grad,
+    tok_hbm, cot_hbm, routes_hbm, comb_hbm, wg_hbm, wu_hbm, wd_hbm, out, grad,
     X, Y, wg, wu, wd, cb, gacc, uacc, bacc, H, G,
-    PO, PG, RcO, RcG, R1O, R2O, RzO, R1G, R2G, RzG, ssem, rsem, lsem,
+    PO, PG, RcO, RcG, R1O, R2O, RzO, R1G, R2G, RzG, ssem, rsem, lsem, routes, comb,
 ):
     e, h = lax.axis_index("expert"), lax.axis_index("hidden")
     z, x, y, c = e // 2, e % 2, h // 2, h % 2
     xn, yn, cn = 1 - x, 1 - y, 1 - c
-    cols = tok.shape[1]
+    cols = tok_hbm.shape[1]
     units = wd_hbm.shape[1]
     dev_x, dev_y, dev_s = (z * 2 + xn, h), (e, yn * 2 + c), (e, y * 2 + cn)
     xf, yf = c * x + (1 - c) * xn, c * yn + (1 - c) * y
@@ -154,16 +154,32 @@
     for dev in partners:
         pl.semaphore_signal(barrier, inc=1, device_id=dev, device_id_type=MESH)
 
-    X[h, rows(x, z), :] = tok[...]
-    Y[h, rows(x, z), :] = cot[...]
-    lane = lax.broadcasted_iota(jnp.int32, (ROWS, 128), 1)
-    expert = jnp.where(lane < 16, lane, lane - 16)
-    dense = jnp.zeros((ROWS, 128), F32)
-    for k in range(routes.shape[1]):
-        dense = dense + jnp.where(expert == routes[:, k : k + 1], comb[:, k : k + 1], 0.0)
-    high = dense.astype(BF16)
-    low = (dense - high.astype(F32)).astype(BF16)
-    cb[rows(x, z), :] = jnp.where(lane < 16, high.astype(F32), low.astype(F32)).astype(BF16)
+    own_in = [
+        pltpu.make_async_copy(routes_hbm, routes, lsem.at[10]),
+        pltpu.make_async_copy(comb_hbm, comb, lsem.at[11]),
+        pltpu.make_async_copy(tok_hbm, X.at[h, rows(x, z), :], lsem.at[12]),
+        pltpu.make_async_copy(cot_hbm, Y.at[h, rows(x, z), :], lsem.at[13]),
+    ]
+    for copy in own_in:
+        copy.start()
+    own_in[0].wait()
+    own_in[1].wait()
+    line = lax.broadcasted_iota(jnp.int32, (128, ROWS), 0)
+    expert = jnp.where(line < 16, line, line - 16)
+    dense = jnp.zeros((128, ROWS), F32)
+    for k in range(routes.shape[0]):
+        dense = dense + jnp.where(expert == routes[k : k + 1, :], comb[k : k + 1, :], 0.0)
+    high = dense.astype(BF16).astype(F32)
+    pair = jnp.where(line < 16, high, dense - high).astype(BF16)
+    unit = jnp.where(
+        lax.broadcasted_iota(jnp.int32, (ROWS, ROWS), 0)
+        == lax.broadcasted_iota(jnp.int32, (ROWS, ROWS), 1),
+        1.0,
+        0.0,
+    ).astype(BF16)
+    cb[rows(x, z), :] = dot_nt(unit, pair).astype(BF16)
+    own_in[2].wait()
+    own_in[3].wait()
     pl.semaphore_wait(barrier, len(partners))
 
     def near(i):
@@ -405,7 +421,7 @@
     width = w_gate.shape[1]
     all_rows = 8 * ROWS
     vmem = pl.BlockSpec(memory_space=pltpu.VMEM)
-    hbm = pl.BlockSpec(memory_space=pl.ANY)
+    hbm = pl.BlockSpec(memory_space=pltpu.HBM)
     bf = lambda *shape: pltpu.VMEM(shape, BF16)
     fl = lambda *shape: pltpu.VMEM(shape, F32)
     flops = 2 * all_rows * 6 * 2 * units * width
@@ -415,7 +431,7 @@
             jax.ShapeDtypeStruct(tokens.shape, BF16),
             jax.ShapeDtypeStruct(tokens.shape, BF16),
         ),
-        in_specs=[vmem] * 4 + [hbm] * 3,
+        in_specs=[hbm] * 7,
         out_specs=(vmem, vmem),
         scratch_shapes=[
             bf(4, all_rows, cols), bf(4, all_rows, cols),
@@ -429,7 +445,9 @@
             bf(2, 4, ROWS, cols), bf(4, ROWS, cols), bf(3, ROWS, cols),
             pltpu.SemaphoreType.DMA((COPIES,)),
             pltpu.SemaphoreType.DMA((COPIES,)),
-            pltpu.SemaphoreType.DMA((10,)),
+            pltpu.SemaphoreType.DMA((14,)),
+            pltpu.VMEM(routes.shape[::-1], jnp.int32),
+            fl(*routes.shape[::-1]),
         ],
         compiler_params=pltpu.CompilerParams(
             collective_id=0, has_side_effects=True, vmem_limit_bytes=52 * 2**20
@@ -437,7 +455,7 @@
         cost_estimate=pl.CostEstimate(
             flops=flops, bytes_accessed=2 * 3 * 2 * units * width, transcendentals=0
         ),
-    )(tokens, cotangent, routes, combine, w_gate, w_up, w_down)
+    )(tokens, cotangent, routes.T, combine.T, w_gate, w_up, w_down)
 
 
 def solution(mesh):

time: 58.1 us -> 58 us (level)
    unnamed x8 -> x10, local copies, waits for them, and re-layouts: 4.4 us -> 4.25 us
where the time goes in v4:
time: 58 us; the launch traced here: 57.8 us
  Pallas kernels  52.9 us (91%)
  local copies, waits for them, and re-layouts  4.25 us (7%)
  between operations  0.65 us (1%)
    pallas_call x1, Pallas kernels, fused(): pl.pallas_call(kernel, out_shape=(jax.ShapeDtypeStruct(tokens.shape, BF16...  52.9 us
    unnamed x10, local copies, waits for them, and re-layouts  4.25 us

profile of v4, /device:TPU:0, one launch (start us, length us, event | category | flops | bytes accessed | tf_op | source)
XLA Modules:
  0.0 57.8 jit_solution(7071449529317509048)
XLA Ops:
  0.6 0.0 copy-start
  0.6 0.8 %copy-done = bf16[16,1792]{1,0:T(8,128)(2,1)S(1)} copy-done((bf16[16,1792]{1,0:T(8,128)(2,1)S(1)}, bf16[16,1792]{1,0:T(8,128)(2,1)}, u32[]{:S(2)}) %copy-start) | copy-done | bytes 57368
  1.5 0.0 copy-start.1
  1.5 0.8 %copy-done.1 = bf16[16,1792]{1,0:T(8,128)(2,1)S(1)} copy-done((bf16[16,1792]{1,0:T(8,128)(2,1)S(1)}, bf16[16,1792]{1,0:T(8,128)(2,1)}, u32[]{:S(2)}) %copy-start.1) | copy-done | bytes 57368
  2.3 0.0 copy-start.2
  2.3 0.7 %copy-done.2 = s32[16,8]{0,1:T(8,128)S(1)} copy-done((s32[16,8]{0,1:T(8,128)S(1)}, s32[16,8]{0,1:T(8,128)}, u32[]{:S(2)}) %copy-start.2) | copy-done | bytes 536
  3.0 0.0 copy-start.3
  3.0 0.7 %copy-done.3 = f32[16,8]{0,1:T(8,128)S(1)} copy-done((f32[16,8]{0,1:T(8,128)S(1)}, f32[16,8]{0,1:T(8,128)}, u32[]{:S(2)}) %copy-start.3) | copy-done | bytes 536
  3.6 52.9 %shard_map.86 = (bf16[16,1792]{1,0:T(8,128)(2,1)S(1)}, bf16[16,1792]{1,0:T(8,128)(2,1)S(1)}) custom-call(bf16[16,1792]{1,0:T(8,128)(2,1)S(1)} %copy-done, bf16[16,1792]{1,0:T(8,128)(2,1)S(1)} %copy-done.1, s32[8,16]{1,0:T(8,128)S(1)} %bitcast.2, f32[8,16]{1,0:T(8,128)S(1)} %bitcast.3, bf16[2,7168,256]{2,1,0:T(8,128)(2,1)} %wg_hbm.1, ...), custom_call_target="tpu_custom_call" | custom-call | flops 5637144576 | bytes 22020096 | tf_op jit(solution)/shard_map/pallas_call | solution.py:428
  56.5 0.6 %copy.11 = bf16[16,1792]{1,0:T(8,128)(2,1)} copy(bf16[16,1792]{1,0:T(8,128)(2,1)S(1)} %get-tuple-element.4) | data formatting | bytes 114688
  57.1 0.6 %copy.12 = bf16[16,1792]{1,0:T(8,128)(2,1)} copy(bf16[16,1792]{1,0:T(8,128)(2,1)S(1)} %get-tuple-element.5) | data formatting | bytes 114688
Async XLA Ops:
  0.6 0.8 %copy-start = (bf16[16,1792]{1,0:T(8,128)(2,1)S(1)}, bf16[16,1792]{1,0:T(8,128)(2,1)}, u32[]{:S(2)}) copy-start(bf16[16,1792]{1,0:T(8,128)(2,1)} %tok_hbm.1) | copy-start | bytes 172036
  1.5 0.8 %copy-start.1 = (bf16[16,1792]{1,0:T(8,128)(2,1)S(1)}, bf16[16,1792]{1,0:T(8,128)(2,1)}, u32[]{:S(2)}) copy-start(bf16[16,1792]{1,0:T(8,128)(2,1)} %cot_hbm.1) | copy-start | bytes 172036
  2.3 0.7 %copy-start.2 = (s32[16,8]{0,1:T(8,128)S(1)}, s32[16,8]{0,1:T(8,128)}, u32[]{:S(2)}) copy-start(s32[16,8]{0,1:T(8,128)} %param.8) | copy-start | bytes 1540
  3.0 0.7 %copy-start.3 = (f32[16,8]{0,1:T(8,128)S(1)}, f32[16,8]{0,1:T(8,128)}, u32[]{:S(2)}) copy-start(f32[16,8]{0,1:T(8,128)} %param.9) | copy-start | bytes 1540
